TPU v7x, 32 devices: a whole 2x2x4 slice. The times are simulated.
32 devices in a mesh: row: 8 (over z, y), col: 4 (over x, core).
Axes of the slice: x: 2, y: 2, z: 4, core: 2. Of those that a mesh axis runs over, the one named last changes fastest.
Arguments:
- a_weights: bfloat16 [4096, 1024], P('row', 'col'), may hold values from 0.0001 to 1, as said below
- tile_mask: int32 [8, 2], replicated, may hold values from 0 to 1, as said below
- pair_mask: int32 [8, 8], replicated, may hold values from 0 to 1, as said below
Outputs:
- jaccard: bfloat16 [4096, 4096], P('row', 'col')
Inputs may be any that keep to these rules, and one draw needn't show every extreme that they name: `a_weights`: all weights positive. `tile_mask`: 1 where a tile is present; tile (I, I mod 2) of every block row I is present. `pair_mask`: symmetric, with ones on the diagonal.
All inputs are finite; a program needn't handle non-finite values.
Results may differ from a plain program's by a relative error of at most 0.001.
Values may be sent and summed in bfloat16 or wider, within the bound.
A program may use at most 64 MiB of HBM per device.

v0:
```python
import jax
import jax.numpy as jnp
from jax import lax
from jax.sharding import PartitionSpec as P

BLOCK = 512


def broadcast(value, axis, source):
    kept = jnp.where(lax.axis_index(axis) == source, value, 0).astype(value.dtype)
    return lax.psum(kept, axis)


def expand_tiles(flags):
    return jnp.repeat(jnp.repeat(flags, BLOCK, axis=0), BLOCK, axis=1)


def body(a_weights, tile_mask, pair_mask):
    row_index = lax.axis_index("row")
    col_index = lax.axis_index("col")
    pair_count = lax.axis_size("row") // lax.axis_size("col")
    blocks_here = a_weights.shape[0] // BLOCK
    own_flags = lax.dynamic_slice_in_dim(tile_mask, row_index * blocks_here, blocks_here, 0)
    own_mask = expand_tiles(own_flags).astype(jnp.bfloat16)
    gathered = lax.all_gather(a_weights, "col", axis=1, tiled=True)
    own_panel = gathered * own_mask
    row_degree = jnp.einsum("ik,ik->i", own_panel, own_panel, preferred_element_type=jnp.float32)
    remotes = [
        broadcast(own_panel, "row", pair_count * col_index + offset) for offset in range(pair_count)
    ]
    outputs = []
    for offset in range(pair_count):
        col_first = (pair_count * col_index + offset) * blocks_here
        remote = remotes[offset]
        pair_tiles = lax.dynamic_slice(
            pair_mask, (row_index * blocks_here, col_first), (blocks_here, blocks_here)
        )
        pair_open = expand_tiles(pair_tiles) > 0
        col_degree = jnp.einsum("ik,ik->i", remote, remote, preferred_element_type=jnp.float32)
        shared = lax.dot_general(
            own_panel, remote, (((1,), (1,)), ((), ())), preferred_element_type=jnp.float32
        )
        weights = shared / (row_degree[:, None] + col_degree[None, :] - shared)
        outputs.append(jnp.where(pair_open, weights, jnp.zeros_like(weights)))
    return jnp.concatenate(outputs, axis=1).astype(jnp.bfloat16)


def solution(mesh):
    in_specs = (P("row", "col"), P(), P())
    out_specs = P("row", "col")
    return jax.shard_map(body, mesh=mesh, in_specs=in_specs, out_specs=out_specs, check_vma=False)
```

profile of v0, /device:TPU:0, one launch (start us, length us, event | category | flops | bytes accessed | tf_op | source)
XLA Modules:
  0.0 146.8 jit_solution(6093091236768662315)
XLA Ops:
  6.5 0.0 all-gather.2.cloned.1.call-start
  6.5 0.7 all-gather.2.cloned.1.call-update
  7.3 0.0 all-reduce.3.cloned.1.call-start
  7.3 0.9 fusion.17
  8.2 0.1 broadcast_bitcast_fusion
  8.3 20.2 %all-gather.2.cloned.1.call-done = bf16[512,1024]{1,0:T(8,128)(2,1)} async-done(((bf16[512,256]{1,0:T(8,128)(2,1)}), bf16[512,1024]{1,0:T(8,128)(2,1)}) %all-gather.2.cloned.1.call-update) | async-done | bytes 1048592 | tf_op jit(solution)/shard_map/all_gather | solution.py:25
  28.5 2.7 %broadcast_select_fusion.1 = (bf16[512,1024]{1,0:T(8,128)(2,1)}, bf16[512,1024]{1,0:T(8,128)(2,1)}) fusion(pred[]{:T(512)S(6)} %eq.6, bf16[512,1024]{1,0:T(8,128)(2,1)} %all-gather.2.cloned.1.call-done, bf16[1024]{0:T(1024)(128)(2,1)S(1)} %bitcast.7, pred[]{:T(512)S(6)} %eq.7), kind=kLoop, calls=%fused_computation.14 | loop fusion | flops 1572864 | bytes 3147778 | tf_op jit(solution)/shard_map/jit(_where)/select_n | solution.py:10
  31.2 0.0 copy-start
  31.2 0.0 all-reduce.3.cloned.1.call-update
  31.2 1.5 fusion.18
  34.0 0.0 copy-done
  34.0 0.3 fusion.2
  34.3 100.0 %all-reduce.3.cloned.1.call-done = (bf16[512,1024]{1,0:T(8,128)(2,1)}, bf16[512,1024]{1,0:T(8,128)(2,1)}) async-done(((bf16[512,1024]{1,0:T(8,128)(2,1)}, bf16[512,1024]{1,0:T(8,128)(2,1)}), (bf16[512,1024]{1,0:T(8,128)(2,1)}, bf16[512,1024]{1,0:T(8,128)(2,1)})) %all-reduce.3.cloned.1.call-update) | async-done | bytes 2097168 | tf_op jit(solution)/shard_map/psum | solution.py:11
  134.4 0.0 copy-start.2
  134.4 2.1 %fusion = (f32[512]{0:T(512)S(1)}, f32[512]{0:T(512)S(1)}) fusion(bf16[512,1024]{1,0:T(8,128)(2,1)} %get-tuple-element.5, bf16[512,1024]{1,0:T(8,128)(2,1)} %get-tuple-element.6), kind=kLoop, calls=%fused_computation.1 | loop fusion | flops 3144704 | bytes 2101248 | tf_op jit(solution)/shard_map/ik,ik->i/dot_general | solution.py:39
  136.5 0.0 copy-done.2
  136.5 0.0 copy-start.1
  136.5 0.8 fusion.4
  137.3 0.4 copy-done.1
  137.7 0.8 fusion.6
  138.5 0.1 pad_maximum_fusion
  138.6 1.3 copy.4
  (1 shorter events, 0.0 us)
Async XLA Ops:
  6.5 21.9 %all-gather.2.cloned.1.call-start = ((), (), s32[]{:S(2)}) async-start(), calls=%async_computation | async-start | bytes 1310720 | tf_op jit(solution)/shard_map/all_gather | solution.py:25
  7.3 127.1 %all-reduce.3.cloned.1.call-start = ((), (), s32[]{:S(2)}) async-start(), calls=%async_computation.1 | async-start | bytes 4194304 | tf_op jit(solution)/shard_map/psum | solution.py:11
  31.2 2.8 %copy-start = (bf16[512,1024]{1,0:T(8,128)(2,1)S(1)}, bf16[512,1024]{1,0:T(8,128)(2,1)}, u32[]{:S(2)}) copy-start(bf16[512,1024]{1,0:T(8,128)(2,1)} %all-gather.2.cloned.1.call-done) | copy-start | bytes 3145732
  134.4 2.1 %copy-start.2 = (bf16[512,1024]{1,0:T(8,128)(2,1)S(1)}, bf16[512,1024]{1,0:T(8,128)(2,1)}, u32[]{:S(2)}) copy-start(bf16[512,1024]{1,0:T(8,128)(2,1)} %get-tuple-element.6) | copy-start | bytes 3145732
  136.5 1.2 copy-start.1
Sparse Core Ops, SparseCore 0:
  8.9 19.5 all-gather.1
  32.1 102.1 all-reduce.2
where the time goes:
time: 147 us
  waiting for transfers between devices  121 us (82%)
  between operations  14.8 us (10%)
  other arithmetic  6.09 us (4%)
  local copies, waits for them, and re-layouts  3.28 us (2%)
  matrix products  1.58 us (1%)
    psum x1, waiting for transfers between devices, broadcast(): return lax.psum(kept, axis)  100 us
    all_gather x1, waiting for transfers between devices, body(): gathered = lax.all_gather(a_weights, 'col', axis=1, tiled=True)  20.2 us
  transfers between devices with their start and end apart: 2, of which 2 were waited for; matrix products, arithmetic and copies ran while one was open for 2% of the time, Pallas kernels for 0%

commit v1 on v0

--- a/solution.py
+++ b/solution.py
@@ -22,7 +22,12 @@
     blocks_here = a_weights.shape[0] // BLOCK
     own_flags = lax.dynamic_slice_in_dim(tile_mask, row_index * blocks_here, blocks_here, 0)
     own_mask = expand_tiles(own_flags).astype(jnp.bfloat16)
-    gathered = lax.all_gather(a_weights, "col", axis=1, tiled=True)
+    ring = [a_weights]
+    for hop in range(3):
+        ring.append(lax.ppermute(ring[-1], "col", [(dev, (dev + 1) % 4) for dev in range(4)]))
+    gathered = jnp.roll(
+        jnp.concatenate(ring[::-1], axis=1), (lax.axis_index("col") + 1) * ring[0].shape[1], axis=1
+    )
     own_panel = gathered * own_mask
     row_degree = jnp.einsum("ik,ik->i", own_panel, own_panel, preferred_element_type=jnp.float32)
     remotes = [

time: 147 us -> 145 us (0.986)
  waiting for transfers between devices: 121 us -> 118 us
    all_gather x1 -> x0, waiting for transfers between devices: 20.2 us -> none  [body(): gathered = lax.all_gather(a_weights, 'col', axis=1, tiled=True)]
    ppermute x0 -> x3, waiting for transfers between devices: none -> 16.9 us  [body(): lax.ppermute(ring[-1], 'col', [(dev, (dev + 1) % 4) for dev in range(4)])]
  transfers between devices with their start and end apart: 2 -> 4, of which waited for: 2 -> 4; matrix products, arithmetic and copies ran while one was open for 2% -> 2% of each run, Pallas kernels for 0% -> 0%
where the time goes in v1:
time: 145 us
  waiting for transfers between devices  118 us (81%)
  between operations  14.8 us (10%)
  other arithmetic  5.22 us (4%)
  local copies, waits for them, and re-layouts  4.42 us (3%)
  matrix products  1.62 us (1%)
    psum x1, waiting for transfers between devices, broadcast(): return lax.psum(kept, axis)  101 us
    ppermute x3, waiting for transfers between devices, body(): lax.ppermute(ring[-1], 'col', [(dev, (dev + 1) % 4) for dev in range(4)])  16.9 us
  transfers between devices with their start and end apart: 4, of which 4 were waited for; matrix products, arithmetic and copies ran while one was open for 2% of the time, Pallas kernels for 0%

profile of v1, /device:TPU:0, one launch (start us, length us, event | category | flops | bytes accessed | tf_op | source)
XLA Modules:
  0.0 144.6 jit_solution(1626656254750767912)
XLA Ops:
  6.5 0.0 copy-start.2
  6.5 0.0 all-reduce.3.cloned.1.call-start
  6.5 0.5 collective-permute-start
  7.0 6.3 %collective-permute-done = bf16[512,256]{1,0:T(8,128)(2,1)S(1)} collective-permute-done((bf16[512,256]{1,0:T(8,128)(2,1)}, bf16[512,256]{1,0:T(8,128)(2,1)S(1)}, u32[]{:S(2)}, u32[]{:S(2)}) %collective-permute-start) | collective-permute-done | bytes 262176 | tf_op jit(solution)/shard_map/ppermute | solution.py:27
  13.3 0.0 collective-permute-start.1
  13.3 5.8 %collective-permute-done.1 = bf16[512,256]{1,0:T(8,128)(2,1)S(1)} collective-permute-done((bf16[512,256]{1,0:T(8,128)(2,1)S(1)}, bf16[512,256]{1,0:T(8,128)(2,1)S(1)}, u32[]{:S(2)}, u32[]{:S(2)}) %collective-permute-start.1) | collective-permute-done | bytes 262176 | tf_op jit(solution)/shard_map/ppermute | solution.py:27
  19.0 0.0 collective-permute-start.2
  19.1 0.9 fusion.9
  19.9 0.1 broadcast_bitcast_fusion
  20.0 4.8 %collective-permute-done.2 = bf16[512,256]{1,0:T(8,128)(2,1)S(1)} collective-permute-done((bf16[512,256]{1,0:T(8,128)(2,1)S(1)}, bf16[512,256]{1,0:T(8,128)(2,1)S(1)}, u32[]{:S(2)}, u32[]{:S(2)}) %collective-permute-start.2) | collective-permute-done | bytes 262176 | tf_op jit(solution)/shard_map/ppermute | solution.py:27
  24.9 1.0 constant_dynamic-update-slice_fusion.4
  26.0 0.0 copy-done.2
  26.1 1.8 %broadcast_select_fusion.1 = (bf16[512,1024]{1,0:T(8,128)(2,1)}, bf16[512,1024]{1,0:T(8,128)(2,1)}) fusion(pred[]{:T(512)S(6)} %eq.9, bf16[1024]{0:T(1024)(128)(2,1)S(1)} %bitcast.7, bf16[512,2048]{1,0:T(8,128)(2,1)S(1)} %constant_dynamic-update-slice_fusion, s32[]{:T(128)S(6)} %select_n.48, pred[]{:T(512)S(6)} %eq.10), kind=kLoop, calls=%fused_computation.15 | loop fusion | flops 3145728 | bytes 3147782 | tf_op jit(solution)/shard_map/jit(_where)/select_n | solution.py:10
  27.9 0.0 all-reduce.3.cloned.1.call-update
  27.9 1.4 fusion.12
  30.6 0.4 fusion.2
  31.0 101.2 %all-reduce.3.cloned.1.call-done = (bf16[512,1024]{1,0:T(8,128)(2,1)}, bf16[512,1024]{1,0:T(8,128)(2,1)}) async-done(((bf16[512,1024]{1,0:T(8,128)(2,1)}, bf16[512,1024]{1,0:T(8,128)(2,1)}), (bf16[512,1024]{1,0:T(8,128)(2,1)}, bf16[512,1024]{1,0:T(8,128)(2,1)})) %all-reduce.3.cloned.1.call-update) | async-done | bytes 2097168 | tf_op jit(solution)/shard_map/psum | solution.py:11
  132.2 0.0 copy-start.1
  132.2 2.1 %fusion = (f32[512]{0:T(512)S(1)}, f32[512]{0:T(512)S(1)}) fusion(bf16[512,1024]{1,0:T(8,128)(2,1)} %get-tuple-element.5, bf16[512,1024]{1,0:T(8,128)(2,1)} %get-tuple-element.6), kind=kLoop, calls=%fused_computation.1 | loop fusion | flops 3144704 | bytes 2101248 | tf_op jit(solution)/shard_map/ik,ik->i/dot_general | solution.py:44
  134.3 0.0 copy-done.1
  134.3 0.0 copy-start
  134.3 0.8 fusion.4
  135.1 0.4 copy-done
  135.5 0.8 fusion.6
  136.4 0.1 pad_maximum_fusion
  136.4 1.3 copy.4
  (8 shorter events, 0.2 us)
Async XLA Ops:
  6.5 19.5 %copy-start.2 = (bf16[512,256]{1,0:T(8,128)(2,1)S(1)}, bf16[512,256]{1,0:T(8,128)(2,1)}, u32[]{:S(2)}) copy-start(bf16[512,256]{1,0:T(8,128)(2,1)} %param.3) | copy-start | bytes 786436
  6.5 125.7 %all-reduce.3.cloned.1.call-start = ((), (), s32[]{:S(2)}) async-start(), calls=%async_computation | async-start | bytes 4194304 | tf_op jit(solution)/shard_map/psum | solution.py:11
  6.5 6.7 %collective-permute-start = (bf16[512,256]{1,0:T(8,128)(2,1)}, bf16[512,256]{1,0:T(8,128)(2,1)S(1)}, u32[]{:S(2)}, u32[]{:S(2)}) collective-permute-start(bf16[512,256]{1,0:T(8,128)(2,1)} %param.3), channel_id=1, source_target_pairs={{0,1},{1,2},{2,3},{3,0},{4,5},{5,6},{6,7},{7,4},{8,9},{9,10},{10,1... | collective-permute-start | bytes 786440 | tf_op jit(solution)/shard_map/ppermute | solution.py:27
  13.3 5.8 %collective-permute-start.1 = (bf16[512,256]{1,0:T(8,128)(2,1)S(1)}, bf16[512,256]{1,0:T(8,128)(2,1)S(1)}, u32[]{:S(2)}, u32[]{:S(2)}) collective-permute-start(bf16[512,256]{1,0:T(8,128)(2,1)S(1)} %collective-permute-done), channel_id=1, source_target_pairs={{0,1},{1,2},{2,3},{3,0},{4,5},{5,6},{6,7},{7,4},{8,9},{9,10},{10,1... | collective-permute-start | bytes 786440 | tf_op jit(solution)/shard_map/ppermute | solution.py:27
  19.0 5.8 %collective-permute-start.2 = (bf16[512,256]{1,0:T(8,128)(2,1)S(1)}, bf16[512,256]{1,0:T(8,128)(2,1)S(1)}, u32[]{:S(2)}, u32[]{:S(2)}) collective-permute-start(bf16[512,256]{1,0:T(8,128)(2,1)S(1)} %collective-permute-done.1), channel_id=1, source_target_pairs={{0,1},{1,2},{2,3},{3,0},{4,5},{5,6},{6,7},{7,4},{8,9},{9,10},{10,1... | collective-permute-start | bytes 786440 | tf_op jit(solution)/shard_map/ppermute | solution.py:27
  132.2 2.1 %copy-start.1 = (bf16[512,1024]{1,0:T(8,128)(2,1)S(1)}, bf16[512,1024]{1,0:T(8,128)(2,1)}, u32[]{:S(2)}) copy-start(bf16[512,1024]{1,0:T(8,128)(2,1)} %get-tuple-element.6) | copy-start | bytes 3145732
  134.3 1.2 copy-start
Sparse Core Ops, SparseCore 0:
  28.1 104.0 all-reduce.2
